TPU v7x, 128 devices: a whole 4x4x4 slice. The times are simulated.
128 devices in a mesh: seq: 8 (over z, y_hi), ctx: 16 (over x, y_lo, core).
Axes of the slice: x: 4, y: 4 (y_hi: 2, y_lo: 2; y = y_hi * 2 + y_lo), z: 4, core: 2. Of those that a mesh axis runs over, the one named last changes fastest.
Arguments:
- layer_input: bfloat16 [8, 2048, 2048], P('seq', 'ctx'), may hold values from -6 to 6
- out_cotangent: bfloat16 [8, 2048, 2048], P('seq', 'ctx'), may hold values from -6 to 6
- positions: int32 [8, 2048], P('seq'), may hold values from 0 to 4094, as said below
- qkv_weight: float32 [2048, 2560], P(('seq', 'ctx')), may hold values from -0.15625 to 0.15625
- qkv_first: float32 [2048, 2560], P(('seq', 'ctx')), may hold values from -160 to 160
- qkv_second: float32 [2048, 2560], P(('seq', 'ctx')), may hold values from 3473.408 to 13762.56
- proj_weight: float32 [2048, 2048], P(('seq', 'ctx')), may hold values from -1 to 1
- proj_first: float32 [2048, 2048], P(('seq', 'ctx')), may hold values from -16 to 16
- proj_second: float32 [2048, 2048], P(('seq', 'ctx')), may hold values from 26.712 to 105.84
- gate_up_weight: float32 [2048, 11264], P(('seq', 'ctx')), may hold values from -0.125 to 0.125
- gate_up_first: float32 [2048, 11264], P(('seq', 'ctx')), may hold values from -80 to 80
- gate_up_second: float32 [2048, 11264], P(('seq', 'ctx')), may hold values from 868.352 to 3440.64
- down_weight: float32 [5632, 2048], P(('seq', 'ctx')), may hold values from -0.125 to 0.125
- down_first: float32 [5632, 2048], P(('seq', 'ctx')), may hold values from -48 to 48
- down_second: float32 [5632, 2048], P(('seq', 'ctx')), may hold values from 303.9232 to 1204.224
- norm_gains: float32 [2048, 2], P(('seq', 'ctx')), may hold values from 0.5 to 1.5
- gains_first: float32 [2048, 2], P(('seq', 'ctx')), may hold values from -256 to 256
- gains_second: float32 [2048, 2], P(('seq', 'ctx')), may hold values from 7815.168 to 30965.76
Outputs:
- block_output: bfloat16 [8, 2048, 2048], P('seq', 'ctx')
- input_grad: float32 [8, 2048, 2048], P('seq', 'ctx')
- qkv_first_new: float32 [2048, 2560], P(('seq', 'ctx'))
- qkv_second_new: float32 [2048, 2560], P(('seq', 'ctx'))
- qkv_weight_new: float32 [2048, 2560], P(('seq', 'ctx'))
- proj_first_new: float32 [2048, 2048], P(('seq', 'ctx'))
- proj_second_new: float32 [2048, 2048], P(('seq', 'ctx'))
- proj_weight_new: float32 [2048, 2048], P(('seq', 'ctx'))
- gate_up_first_new: float32 [2048, 11264], P(('seq', 'ctx'))
- gate_up_second_new: float32 [2048, 11264], P(('seq', 'ctx'))
- gate_up_weight_new: float32 [2048, 11264], P(('seq', 'ctx'))
- down_first_new: float32 [5632, 2048], P(('seq', 'ctx'))
- down_second_new: float32 [5632, 2048], P(('seq', 'ctx'))
- down_weight_new: float32 [5632, 2048], P(('seq', 'ctx'))
- gains_first_new: float32 [2048, 2], P(('seq', 'ctx'))
- gains_second_new: float32 [2048, 2], P(('seq', 'ctx'))
- gains_new: float32 [2048, 2], P(('seq', 'ctx'))
Inputs may be any that keep to these rules, and one draw needn't show every extreme that they name: Along each sequence's own order the positions start at 0 and rise strictly from token to token, by 1 or 2 except at the last token, which sits at 4094. The array holds each sequence in 32 blocks of 64 tokens; the two blocks stored at slots 2c and 2c+1 are blocks b and 31-b of the sequence's order for some b, in either order.
All inputs are finite; a program needn't handle non-finite values.
Results may differ from a plain program's by a relative error of at most 0.022.
Values may be sent and summed in bfloat16 or wider, within the bound.
No kernel may reach another device: no remote copies, remote signals or barrier semaphores. Data moves between devices by JAX's collectives and lax.ppermute only.
A program may use at most 448 MiB of HBM per device.

v0:
```python
import jax
import jax.numpy as jnp
from jax import lax
from jax.sharding import PartitionSpec as P

HEADS = 32
KV_HEADS = 4
HEAD_DIM = 64
STEP = 10


norm_eps = 1e-05
rope_base = 10000.0
beta_one = 0.9
beta_two = 0.95
adam_eps = 1e-08
decay_rate = 0.1
rate_qkv = 0.05
rate_proj = 0.3
rate_gate_up = 0.04
rate_down = 0.04
rate_gains = 0.5


def rotary_tables(token_pos, half_dim):
    inv_freq = rope_base ** (-jnp.arange(half_dim, dtype=jnp.float32) * 2.0 / (2 * half_dim))
    angles = token_pos.astype(jnp.float32)[:, None] * inv_freq[None, :]
    return (jnp.cos(angles), jnp.sin(angles))


def rotate(field, cos_vals, sin_vals):
    half_dim = field.shape[-1] // 2
    first_half = field[..., :half_dim]
    second_half = field[..., half_dim:]
    cos_b = cos_vals[:, None, :]
    sin_b = sin_vals[:, None, :]
    return jnp.concatenate(
        [first_half * cos_b - second_half * sin_b, second_half * cos_b + first_half * sin_b],
        axis=-1,
    )


def unrotate(field, cos_vals, sin_vals):
    half_dim = field.shape[-1] // 2
    first_half = field[..., :half_dim]
    second_half = field[..., half_dim:]
    cos_b = cos_vals[:, None, :]
    sin_b = sin_vals[:, None, :]
    return jnp.concatenate(
        [first_half * cos_b + second_half * sin_b, second_half * cos_b - first_half * sin_b],
        axis=-1,
    )


def norm_rows(field, gain_vals):
    scale_vals = lax.rsqrt(jnp.mean(field * field, axis=-1, keepdims=True) + norm_eps)
    normed = field * scale_vals
    return (normed, scale_vals, normed * gain_vals[None, :])


def norm_back(grad_out, normed, scale_vals, gain_vals):
    grad_normed = grad_out * gain_vals[None, :]
    row_inner = jnp.mean(grad_normed * normed, axis=-1, keepdims=True)
    return (scale_vals * (grad_normed - normed * row_inner), jnp.sum(grad_out * normed, axis=0))


def allowed_mask(own_pos, all_pos, group_size):
    tok_rows = own_pos.shape[0]
    allowed = all_pos[None, :] <= own_pos[:, None]
    return jnp.broadcast_to(allowed[None], (group_size, tok_rows, all_pos.shape[0])).reshape(
        group_size * tok_rows, all_pos.shape[0]
    )


def head_scores(q_head, k_head, allowed):
    scale_vals = q_head.shape[-1] ** (-0.5)
    scores = (
        jnp.einsum("rd,kd->rk", q_head, k_head, preferred_element_type=jnp.float32) * scale_vals
    )
    return jnp.where(allowed, scores, -1e30)


def attend_forward(query_heads, key_heads, value_heads, allowed):

    def one_head(head_args):
        q_head, k_head, v_head = head_args
        scores = head_scores(q_head, k_head, allowed)
        row_top = jnp.max(scores, axis=-1, keepdims=True)
        exp_vals = jnp.exp(scores - row_top)
        row_total = jnp.sum(exp_vals, axis=-1, keepdims=True)
        prob_vals = (exp_vals / row_total).astype(jnp.bfloat16)
        attended = jnp.dot(prob_vals, v_head, preferred_element_type=jnp.float32)
        return (attended, (row_top + jnp.log(row_total))[:, 0])

    return lax.map(one_head, (query_heads, key_heads, value_heads))


def attend_backward(query_heads, key_heads, value_heads, grad_heads, log_sums, allowed):
    scale_vals = query_heads.shape[-1] ** (-0.5)

    def one_head(head_args):
        q_head, k_head, v_head, g_head, l_head = head_args
        scores = head_scores(q_head, k_head, allowed)
        prob_vals = jnp.exp(scores - l_head[:, None])
        grad_probs = jnp.einsum("rd,kd->rk", g_head, v_head, preferred_element_type=jnp.float32)
        row_inner = jnp.sum(prob_vals * grad_probs, axis=-1, keepdims=True)
        grad_scores = (prob_vals * (grad_probs - row_inner)).astype(jnp.bfloat16)
        grad_query = jnp.dot(grad_scores, k_head, preferred_element_type=jnp.float32) * scale_vals
        grad_key = (
            jnp.einsum("rk,rd->kd", grad_scores, q_head, preferred_element_type=jnp.float32)
            * scale_vals
        )
        grad_value = jnp.einsum(
            "rk,rd->kd", prob_vals.astype(jnp.bfloat16), g_head, preferred_element_type=jnp.float32
        )
        return (grad_query, grad_key, grad_value)

    return lax.map(one_head, (query_heads, key_heads, value_heads, grad_heads, log_sums))


def adam_step(weight, moment_one, moment_two, gradient, step_rate, weight_decay):
    first_new = beta_one * moment_one + (1.0 - beta_one) * gradient
    second_new = beta_two * moment_two + (1.0 - beta_two) * gradient * gradient
    first_hat = first_new / (1.0 - beta_one**STEP)
    second_hat = second_new / (1.0 - beta_two**STEP)
    weight_new = weight - step_rate * (
        first_hat / (jnp.sqrt(second_hat) + adam_eps) + weight_decay * weight
    )
    return (first_new, second_new, weight_new)


def on_device(
    layer_input,
    out_cotangent,
    positions,
    qkv_weight,
    qkv_first,
    qkv_second,
    proj_weight,
    proj_first,
    proj_second,
    gate_up_weight,
    gate_up_first,
    gate_up_second,
    down_weight,
    down_first,
    down_second,
    norm_gains,
    gains_first,
    gains_second,
):
    tok_rows = layer_input.shape[1]
    group_size = HEADS // KV_HEADS
    q_cols = HEADS * HEAD_DIM
    k_cols = KV_HEADS * HEAD_DIM
    all_pos = positions[0]
    own_pos = lax.dynamic_slice_in_dim(all_pos, lax.axis_index("ctx") * tok_rows, tok_rows)
    cos_vals, sin_vals = rotary_tables(own_pos, HEAD_DIM // 2)
    allowed = allowed_mask(own_pos, all_pos, group_size)
    inputs = layer_input[0].astype(jnp.float32)
    qkv_full, proj_full, gains_full = (
        lax.all_gather(qkv_weight.astype(jnp.bfloat16), ("seq", "ctx"), axis=0, tiled=True),
        lax.all_gather(proj_weight.astype(jnp.bfloat16), ("seq", "ctx"), axis=0, tiled=True),
        lax.all_gather(norm_gains.astype(jnp.bfloat16), ("seq", "ctx"), axis=0, tiled=True),
    )
    gain_vals = gains_full.astype(jnp.float32)
    normed_one, scale_one, pre_one = norm_rows(inputs, gain_vals[:, 0])
    hidden_one = pre_one.astype(jnp.bfloat16)
    projected = jnp.dot(hidden_one, qkv_full, preferred_element_type=jnp.float32)
    queries = rotate(
        projected[:, :q_cols].reshape(tok_rows, HEADS, HEAD_DIM), cos_vals, sin_vals
    ).astype(jnp.bfloat16)
    key_rows = (
        rotate(
            projected[:, q_cols : q_cols + k_cols].reshape(tok_rows, KV_HEADS, HEAD_DIM),
            cos_vals,
            sin_vals,
        )
        .astype(jnp.bfloat16)
        .reshape(tok_rows, k_cols)
    )
    values = projected[:, q_cols + k_cols :].astype(jnp.bfloat16)
    keys_all, values_all = (
        lax.all_gather(key_rows, "ctx", axis=0, tiled=True),
        lax.all_gather(values, "ctx", axis=0, tiled=True),
    )
    length = keys_all.shape[0]
    query_heads = (
        queries.reshape(tok_rows, KV_HEADS, group_size, HEAD_DIM)
        .transpose(1, 2, 0, 3)
        .reshape(KV_HEADS, group_size * tok_rows, HEAD_DIM)
    )
    key_heads = keys_all.reshape(length, KV_HEADS, HEAD_DIM).transpose(1, 0, 2)
    value_heads = values_all.reshape(length, KV_HEADS, HEAD_DIM).transpose(1, 0, 2)
    attended, log_sums = attend_forward(query_heads, key_heads, value_heads, allowed)
    merged = (
        attended.reshape(KV_HEADS, group_size, tok_rows, HEAD_DIM)
        .transpose(2, 0, 1, 3)
        .reshape(tok_rows, q_cols)
        .astype(jnp.bfloat16)
    )
    middle = inputs + jnp.dot(merged, proj_full, preferred_element_type=jnp.float32)
    normed_two, scale_two, pre_two = norm_rows(middle, gain_vals[:, 1])
    hidden_two = pre_two.astype(jnp.bfloat16)
    gate_up_use, down_use = (
        lax.all_gather(gate_up_weight.astype(jnp.bfloat16), ("seq", "ctx"), axis=0, tiled=True),
        lax.all_gather(down_weight.astype(jnp.bfloat16), ("seq", "ctx"), axis=0, tiled=True),
    )
    hidden_units = gate_up_use.shape[1] // 2
    gate_up = jnp.dot(hidden_two, gate_up_use, preferred_element_type=jnp.float32)
    gate_vals = gate_up[:, :hidden_units]
    up_vals = gate_up[:, hidden_units:]
    sig_vals = jax.nn.sigmoid(gate_vals)
    activated = gate_vals * sig_vals
    product = (activated * up_vals).astype(jnp.bfloat16)
    branch_terms = jnp.dot(product, down_use, preferred_element_type=jnp.float32)
    result = middle + branch_terms
    grad_result = out_cotangent[0].astype(jnp.float32)
    grad_branch = grad_result.astype(jnp.bfloat16)
    grad_down_term = jnp.einsum(
        "tf,td->fd", product, grad_branch, preferred_element_type=jnp.float32
    )
    grad_product = jnp.einsum(
        "td,fd->tf", grad_branch, down_use, preferred_element_type=jnp.float32
    )
    grad_gate = grad_product * up_vals * (sig_vals * (1.0 + gate_vals * (1.0 - sig_vals)))
    grad_up = grad_product * activated
    grad_gate_up = jnp.concatenate([grad_gate, grad_up], axis=1).astype(jnp.bfloat16)
    grad_gate_up_term = jnp.einsum(
        "td,tf->df", hidden_two, grad_gate_up, preferred_element_type=jnp.float32
    )
    hidden_terms = jnp.einsum(
        "tf,df->td", grad_gate_up, gate_up_use, preferred_element_type=jnp.float32
    )
    sum_gate_up, sum_down = (
        lax.psum_scatter(grad_gate_up_term, ("seq", "ctx"), scatter_dimension=0, tiled=True),
        lax.psum_scatter(grad_down_term, ("seq", "ctx"), scatter_dimension=0, tiled=True),
    )
    grad_mid_norm, grad_gain_two = norm_back(hidden_terms, normed_two, scale_two, gain_vals[:, 1])
    grad_middle = grad_result + grad_mid_norm
    grad_attn_branch = grad_middle.astype(jnp.bfloat16)
    grad_proj_term = jnp.einsum(
        "tq,td->qd", merged, grad_attn_branch, preferred_element_type=jnp.float32
    )
    grad_merged = jnp.einsum(
        "td,qd->tq", grad_attn_branch, proj_full, preferred_element_type=jnp.float32
    ).astype(jnp.bfloat16)
    grad_heads = (
        grad_merged.reshape(tok_rows, KV_HEADS, group_size, HEAD_DIM)
        .transpose(1, 2, 0, 3)
        .reshape(KV_HEADS, group_size * tok_rows, HEAD_DIM)
    )
    grad_query, grad_key, grad_value = attend_backward(
        query_heads, key_heads, value_heads, grad_heads, log_sums, allowed
    )
    grad_key_flat = grad_key.transpose(1, 0, 2).reshape(length, k_cols)
    grad_value_flat = grad_value.transpose(1, 0, 2).reshape(length, k_cols)
    own_key_grad, own_value_grad = (
        lax.psum_scatter(
            grad_key_flat.astype(jnp.bfloat16), "ctx", scatter_dimension=0, tiled=True
        ).astype(jnp.float32),
        lax.psum_scatter(
            grad_value_flat.astype(jnp.bfloat16), "ctx", scatter_dimension=0, tiled=True
        ).astype(jnp.float32),
    )
    grad_query_rows = (
        grad_query.reshape(KV_HEADS, group_size, tok_rows, HEAD_DIM)
        .transpose(2, 0, 1, 3)
        .reshape(tok_rows, HEADS, HEAD_DIM)
    )
    grad_query_raw = unrotate(grad_query_rows, cos_vals, sin_vals).reshape(tok_rows, q_cols)
    grad_key_raw = unrotate(
        own_key_grad.reshape(tok_rows, KV_HEADS, HEAD_DIM), cos_vals, sin_vals
    ).reshape(tok_rows, k_cols)
    grad_projected = jnp.concatenate([grad_query_raw, grad_key_raw, own_value_grad], axis=1).astype(
        jnp.bfloat16
    )
    grad_qkv_term = jnp.einsum(
        "td,tc->dc", hidden_one, grad_projected, preferred_element_type=jnp.float32
    )
    grad_hidden_one = jnp.einsum(
        "tc,dc->td", grad_projected, qkv_full, preferred_element_type=jnp.float32
    )
    grad_in_norm, grad_gain_one = norm_back(grad_hidden_one, normed_one, scale_one, gain_vals[:, 0])
    input_grad = grad_middle + grad_in_norm
    grad_gains_term = jnp.stack([grad_gain_one, grad_gain_two], axis=1)
    sum_qkv, sum_proj, sum_gains = (
        lax.psum_scatter(grad_qkv_term, ("seq", "ctx"), scatter_dimension=0, tiled=True),
        lax.psum_scatter(grad_proj_term, ("seq", "ctx"), scatter_dimension=0, tiled=True),
        lax.psum_scatter(grad_gains_term, ("seq", "ctx"), scatter_dimension=0, tiled=True),
    )
    qkv_new = adam_step(qkv_weight, qkv_first, qkv_second, sum_qkv, rate_qkv, decay_rate)
    proj_new = adam_step(proj_weight, proj_first, proj_second, sum_proj, rate_proj, decay_rate)
    gate_up_new = adam_step(
        gate_up_weight, gate_up_first, gate_up_second, sum_gate_up, rate_gate_up, decay_rate
    )
    down_new = adam_step(down_weight, down_first, down_second, sum_down, rate_down, decay_rate)
    gains_new = adam_step(norm_gains, gains_first, gains_second, sum_gains, rate_gains, 0.0)
    return (
        result.astype(jnp.bfloat16)[None],
        input_grad[None],
        qkv_new[0],
        qkv_new[1],
        qkv_new[2],
        proj_new[0],
        proj_new[1],
        proj_new[2],
        gate_up_new[0],
        gate_up_new[1],
        gate_up_new[2],
        down_new[0],
        down_new[1],
        down_new[2],
        gains_new[0],
        gains_new[1],
        gains_new[2],
    )


def solution(mesh):
    return jax.shard_map(
        on_device,
        mesh=mesh,
        in_specs=(
            P("seq", "ctx", None),
            P("seq", "ctx", None),
            P("seq", None),
            P(("seq", "ctx"), None),
            P(("seq", "ctx"), None),
            P(("seq", "ctx"), None),
            P(("seq", "ctx"), None),
            P(("seq", "ctx"), None),
            P(("seq", "ctx"), None),
            P(("seq", "ctx"), None),
            P(("seq", "ctx"), None),
            P(("seq", "ctx"), None),
            P(("seq", "ctx"), None),
            P(("seq", "ctx"), None),
            P(("seq", "ctx"), None),
            P(("seq", "ctx"), None),
            P(("seq", "ctx"), None),
            P(("seq", "ctx"), None),
        ),
        out_specs=(
            P("seq", "ctx", None),
            P("seq", "ctx", None),
            P(("seq", "ctx"), None),
            P(("seq", "ctx"), None),
            P(("seq", "ctx"), None),
            P(("seq", "ctx"), None),
            P(("seq", "ctx"), None),
            P(("seq", "ctx"), None),
            P(("seq", "ctx"), None),
            P(("seq", "ctx"), None),
            P(("seq", "ctx"), None),
            P(("seq", "ctx"), None),
            P(("seq", "ctx"), None),
            P(("seq", "ctx"), None),
            P(("seq", "ctx"), None),
            P(("seq", "ctx"), None),
            P(("seq", "ctx"), None),
        ),
        check_vma=False,
    )
```

profile of v0, /device:TPU:0, one launch (start us, length us, event | category | flops | bytes accessed | tf_op | source)
XLA Modules:
  0.0 4262.2 jit_solution(17302899124678589465)
XLA Ops:
  9.6 178.0 %all-gather = bf16[128,16,2]{1,2,0:T(2,128)(2,1)S(1)} all-gather(bf16[1,16,2]{1,2,0:T(2,128)(2,1)S(1)} %convert_bitcast_fusion.1), channel_id=1, replica_groups=mesh['seq'=8,'ctx'=16] {'seq','ctx'}, dimensions={0}, use_global_device_ids=true | all-gather | bytes 8256 | tf_op jit(solution)/shard_map/all_gather | solution.py:164
  190.1 29.7 all-gather.9.cloned.1.call-done
  232.7 26.2 all-gather.11.cloned.1.call-done
  261.4 32.3 all-gather.13.cloned.1.call-done
  298.8 48.3 %while.30 = (s32[]{:T(128)}, bf16[4,1024,64]{1,2,0:T(8,128)(2,1)}, f32[4,1024]{1,0:T(4,128)S(1)}, bf16[4,1024,64]{2,1,0:T(8,128)(2,1)}, bf16[4,2048,64]{2,1,0:T(...) while((s32[]{:T(128)}, bf16[4,1024,64]{1,2,0:T(8,128)(2,1)}, ...), condition=%wide.region_4.5_spmd.clone.clone, body=%wide.region_1.4_spmd.clone.sunk.clone | while | flops 562035712 | bytes 40151184 | solution.py:95
  349.2 150.1 %all-gather.15.cloned.1.call-done = bf16[2048,2048]{1,0:T(8,128)(2,1)} async-done(((bf16[16,2048]{1,0:T(8,128)(2,1)}), bf16[2048,2048]{1,0:T(8,128)(2,1)}) %all-gather.15.cloned.1.call-update) | async-done | bytes 8388624 | tf_op jit(solution)/shard_map/all_gather | solution.py:163
  505.1 222.2 %all-gather.19.cloned.1.call-done = bf16[128,44,2048]{2,1,0:T(8,128)(2,1)} async-done(((bf16[1,44,2048]{2,1,0:T(8,128)(2,1)}), bf16[128,44,2048]{2,1,0:T(8,128)(2,1)}) %all-gather.19.cloned.1.call-update) | async-done | bytes 23068688 | tf_op jit(solution)/shard_map/all_gather | solution.py:207
  727.3 30.2 reshape.258
  757.5 230.9 %all-gather.17.cloned.1.call-done = bf16[2048,11264]{1,0:T(8,128)(2,1)} async-done(((bf16[16,11264]{1,0:T(8,128)(2,1)}), bf16[2048,11264]{1,0:T(8,128)(2,1)}) %all-gather.17.cloned.1.call-update) | async-done | bytes 46137360 | tf_op jit(solution)/shard_map/all_gather | solution.py:206
  988.4 20.4 fusion.82
  1008.8 14.8 multiply_convert_fusion.2
  1023.6 22.3 multiply_reduce_fusion.1
  1058.4 67.3 %while.31 = (s32[]{:T(128)}, f32[4,1024,64]{1,2,0:T(8,128)}, bf16[4,2048,64]{1,2,0:T(8,128)(2,1)}, bf16[4,2048,64]{1,2,0:T(8,128)(2,1)}, bf16[4,1024,64]{2,1,0:T...) while((s32[]{:T(128)}, f32[4,1024,64]{1,2,0:T(8,128)}, ...), condition=%wide.region_9.10_spmd.clone.clone, body=%wide.region_7.9_spmd.clone.sunk.clone | while | flops 1367538688 | bytes 75789480 | solution.py:118
  1130.9 57.4 %reduce-scatter.21.cloned.1.call-done = bf16[128,256]{1,0:T(8,128)(2,1)} async-done(((bf16[2048,256]{1,0:T(8,128)(2,1)}), bf16[128,256]{1,0:T(8,128)(2,1)}) %reduce-scatter.21.cloned.1.call-update) | async-done | bytes 65552
  1189.3 62.0 %reduce-scatter.23.cloned.1.call-done = bf16[128,256]{1,0:T(8,128)(2,1)} async-done(((bf16[2048,256]{1,0:T(8,128)(2,1)}), bf16[128,256]{1,0:T(8,128)(2,1)}) %reduce-scatter.23.cloned.1.call-update) | async-done | bytes 65552
  1281.7 33.6 fusion.47
  1316.4 19.2 fusion.62
  1335.6 543.0 %fusion.4 = f32[48,2048]{1,0:T(8,128)S(1)} fusion(f32[5632,2048]{1,0:T(8,128)} %fusion.62), kind=kCustom, calls=%all-reduce-scatter | all-reduce-scatter fusion | flops 12582913 | bytes 46530560
  1918.3 25.6 collective-permute-start.2
  1960.8 12.7 collective-permute-done.2
  1986.0 30.8 concatenate.37
  2023.4 567.2 %reduce-scatter.17.cloned.1.call-done = f32[16,2048]{1,0:T(8,128)} async-done(((f32[2048,2048]{1,0:T(8,128)}), f32[16,2048]{1,0:T(8,128)}) %reduce-scatter.17.cloned.1.call-update) | async-done | bytes 131088 | tf_op jit(solution)/shard_map/reduce_scatter | solution.py:289
  2592.4 669.6 %reduce-scatter.15.cloned.1.call-done = f32[16,2560]{1,0:T(8,128)} async-done(((f32[2048,2560]{1,0:T(8,128)}), f32[16,2560]{1,0:T(8,128)}) %reduce-scatter.15.cloned.1.call-update) | async-done | bytes 163856 | tf_op jit(solution)/shard_map/reduce_scatter | solution.py:288
  3263.9 988.3 %reduce-scatter.19.cloned.1.call-done = f32[16,11264]{1,0:T(8,128)} async-done(((f32[2048,11264]{1,0:T(8,128)}), f32[16,11264]{1,0:T(8,128)}) %reduce-scatter.19.cloned.1.call-update) | async-done | bytes 720912 | tf_op jit(solution)/shard_map/reduce_scatter | solution.py:236
  (267 shorter events, 280.0 us)
Async XLA Ops:
  7.2 212.6 %all-gather.9.cloned.1.call-start = ((), (), s32[]{:S(2)}) async-start(), calls=%async_computation.6 | async-start | bytes 10567680 | tf_op jit(solution)/shard_map/all_gather | solution.py:162
  8.8 250.1 %all-gather.11.cloned.1.call-start = ((), (), s32[]{:S(2)}) async-start(), calls=%async_computation.7 | async-start | bytes 1114112 | tf_op jit(solution)/shard_map/all_gather | solution.py:184
  226.4 67.3 %all-gather.13.cloned.1.call-start = ((), (), s32[]{:S(2)}) async-start(), calls=%async_computation.8 | async-start | bytes 1114112 | tf_op jit(solution)/shard_map/all_gather | solution.py:185
  227.2 272.1 %all-gather.15.cloned.1.call-start = ((), (), s32[]{:S(2)}) async-start(), calls=%async_computation.9 | async-start | bytes 8454144 | tf_op jit(solution)/shard_map/all_gather | solution.py:163
  227.9 499.5 %all-gather.19.cloned.1.call-start = ((), (), s32[]{:S(2)}) async-start(), calls=%async_computation.14 | async-start | bytes 25362432 | tf_op jit(solution)/shard_map/all_gather | solution.py:207
  228.7 759.7 %all-gather.17.cloned.1.call-start = ((), (), s32[]{:S(2)}) async-start(), calls=%async_computation.10 | async-start | bytes 46497792 | tf_op jit(solution)/shard_map/all_gather | solution.py:206
  229.5 958.8 %reduce-scatter.21.cloned.1.call-start = ((), (), s32[]{:S(2)}) async-start(), calls=%async_computation.15 | async-start | bytes 1114112
  1128.1 123.2 %reduce-scatter.23.cloned.1.call-start = ((), (), s32[]{:S(2)}) async-start(), calls=%async_computation.16 | async-start | bytes 1114112
  1130.4 891.6 %reduce-scatter.25.cloned.1.call-start = ((), (), s32[]{:S(2)}) async-start(), calls=%async_computation.17 | async-start | bytes 1056768
  1262.4 1328.2 %reduce-scatter.17.cloned.1.call-start = ((), (), s32[]{:S(2)}) async-start(), calls=%async_computation.12 | async-start | bytes 16908288 | tf_op jit(solution)/shard_map/reduce_scatter | solution.py:289
  1271.1 1990.9 %reduce-scatter.15.cloned.1.call-start = ((), (), s32[]{:S(2)}) async-start(), calls=%async_computation.11 | async-start | bytes 21135360 | tf_op jit(solution)/shard_map/reduce_scatter | solution.py:288
  1280.5 2971.7 %reduce-scatter.19.cloned.1.call-start = ((), (), s32[]{:S(2)}) async-start(), calls=%async_computation.13 | async-start | bytes 92995584 | tf_op jit(solution)/shard_map/reduce_scatter | solution.py:236
  1878.6 27.8 collective-permute-start.10
  1884.2 24.3 collective-permute-start.9
  1892.5 17.5 collective-permute-start.8
  1897.2 21.1 collective-permute-start.7
  1904.4 39.4 collective-permute-start.6
  1906.4 38.7 collective-permute-start.5
  1908.5 52.3 %collective-permute-start.4 = (f32[48,2048]{1,0:T(8,128)S(1)}, f32[48,2048]{1,0:T(8,128)S(1)}, u32[]{:S(2)}, u32[]{:S(2)}) collective-permute-start(f32[48,2048]{1,0:T(8,128)S(1)} %fusion.4), channel_id=1, source_target_pairs={{0,5},{1,6},{2,7},{3,8},{4,9},{5,10},{6,11},{7,12},{8,13},{9,14},{... | collective-permute-start | bytes 1179656
  1910.0 50.8 %collective-permute-start.3 = (f32[48,2048]{1,0:T(8,128)S(1)}, f32[48,2048]{1,0:T(8,128)S(1)}, u32[]{:S(2)}, u32[]{:S(2)}) collective-permute-start(f32[48,2048]{1,0:T(8,128)S(1)} %fusion.4), channel_id=1, source_target_pairs={{0,4},{1,5},{2,6},{3,7},{4,8},{5,9},{6,10},{7,11},{8,12},{9,13},{1... | collective-permute-start | bytes 1179656
  1918.3 55.3 %collective-permute-start.2 = (f32[48,2048]{1,0:T(8,128)S(1)}, f32[48,2048]{1,0:T(8,128)S(1)}, u32[]{:S(2)}, u32[]{:S(2)}) collective-permute-start(f32[48,2048]{1,0:T(8,128)S(1)} %fusion.4), channel_id=1, source_target_pairs={{0,3},{1,4},{2,5},{3,6},{4,7},{5,8},{6,9},{7,10},{8,11},{9,12},{10... | collective-permute-start | bytes 1179656
  1943.8 41.4 collective-permute-start.1
  1945.2 40.8 collective-permute-start
  2016.8 2235.4 %copy-start.9 = (f32[16,11264]{1,0:T(8,128)S(1)}, f32[16,11264]{1,0:T(8,128)}, u32[]{:S(2)}) copy-start(f32[16,11264]{1,0:T(8,128)} %param.31) | copy-start | bytes 2162692
  (50 other events, 5961.4 us)
Sparse Core Ops, SparseCore 0:
  10.3 209.4 all-gather.8
  226.6 32.2 all-gather.10
  261.2 32.5 all-gather.12
  295.9 203.2 all-gather.14
  501.4 225.9 all-gather.18
  729.5 258.8 all-gather.16
  1128.2 60.0 reduce-scatter.20
  1191.4 59.9 reduce-scatter.22
  1262.5 638.8 reduce-scatter.24
  1903.8 686.7 reduce-scatter.16
  2593.1 668.7 reduce-scatter.14
  3264.4 987.7 reduce-scatter.18
where the time goes:
time: 4270 us; the launch traced here: 4260 us
  waiting for transfers between devices  3060 us (72%)
  blocking collectives  721 us (17%)
  matrix products  240 us (6%)
  local copies, waits for them, and re-layouts  93.1 us (2%)
  starting transfers between devices  66.9 us (2%)
  other arithmetic  60.8 us (1%)
    reduce_scatter x1, waiting for transfers between devices, on_device(): lax.psum_scatter(grad_gate_up_term, ('seq', 'ctx'), scatter_dimension=0,...  988 us
    reduce_scatter x1, waiting for transfers between devices, on_device(): lax.psum_scatter(grad_qkv_term, ('seq', 'ctx'), scatter_dimension=0, tile...  670 us
    reduce_scatter x1, waiting for transfers between devices, on_device(): lax.psum_scatter(grad_proj_term, ('seq', 'ctx'), scatter_dimension=0, til...  567 us
    unnamed x1, blocking collectives  543 us
    all_gather x1, waiting for transfers between devices, on_device(): lax.all_gather(gate_up_weight.astype(jnp.bfloat16), ('seq', 'ctx'), axis=...  231 us
    all_gather x1, waiting for transfers between devices, on_device(): lax.all_gather(down_weight.astype(jnp.bfloat16), ('seq', 'ctx'), axis=0,...  222 us
    all_gather x1, blocking collectives, on_device(): lax.all_gather(norm_gains.astype(jnp.bfloat16), ('seq', 'ctx'), axis=0, t...  178 us
    all_gather x1, waiting for transfers between devices, on_device(): lax.all_gather(proj_weight.astype(jnp.bfloat16), ('seq', 'ctx'), axis=0,...  150 us
  transfers between devices with their start and end apart: 23, of which 14 were waited for; matrix products, arithmetic and copies ran while one was open for 18% of the time, Pallas kernels for 0%

commit v1 on v0

v1 whole, which is shorter than its diff:
```python
import jax
import jax.numpy as jnp
from jax import lax
from jax.sharding import Mesh
from jax.sharding import PartitionSpec as P

HEADS = 32
KV_HEADS = 4
HEAD_DIM = 64
GROUP = HEADS // KV_HEADS
STEP = 10

norm_eps = 1e-05
rope_base = 10000.0
beta_one = 0.9
beta_two = 0.95
adam_eps = 1e-08
decay_rate = 0.1
rate_qkv = 0.05
rate_proj = 0.3
rate_gate_up = 0.04
rate_down = 0.04
rate_gains = 0.5

SIZES = {"z": 4, "yh": 2, "x": 4, "yl": 2, "c": 2}
SEQ = ("z", "yh")
CTX = ("x", "yl", "c")
ROWS = SEQ + CTX
OWNERS = ("yh", "x", "yl", "c")
RING_Y = ("yh", "yl")
NZ = 4
NCTX = 16
BF = jnp.bfloat16
F32 = jnp.float32


def axis_size(axis):
    if isinstance(axis, str):
        return SIZES[axis]
    count = 1
    for name in axis:
        count *= SIZES[name]
    return count


def send(field, axis, step):
    count = axis_size(axis)
    return lax.ppermute(field, axis, [(i, (i + step) % count) for i in range(count)])


def gather_z(field):
    return [field] + [send(field, "z", step) for step in range(1, NZ)]


def return_z(parts):
    return [send(parts[step], "z", -step) for step in range(1, NZ)]


def dot(lhs, rhs):
    return jnp.dot(lhs, rhs, preferred_element_type=F32)


def dot_t(lhs, rhs):
    return lax.dot_general(lhs, rhs, (((1,), (1,)), ((), ())), preferred_element_type=F32)


def t_dot(lhs, rhs):
    return lax.dot_general(lhs, rhs, (((0,), (0,)), ((), ())), preferred_element_type=F32)


def rotary_tables(token_pos):
    half_dim = HEAD_DIM // 2
    inv_freq = rope_base ** (-jnp.arange(half_dim, dtype=F32) * 2.0 / (2 * half_dim))
    angles = token_pos.astype(F32)[:, None] * inv_freq[None, :]
    return (jnp.cos(angles), jnp.sin(angles))


def rotate(field, cos_vals, sin_vals):
    half_dim = field.shape[-1] // 2
    first_half = field[..., :half_dim]
    second_half = field[..., half_dim:]
    cos_b = cos_vals[:, None, :]
    sin_b = sin_vals[:, None, :]
    return jnp.concatenate(
        [first_half * cos_b - second_half * sin_b, second_half * cos_b + first_half * sin_b],
        axis=-1,
    )


def norm_scale(field):
    return lax.rsqrt(jnp.mean(field * field, axis=-1, keepdims=True) + norm_eps)


def norm_back(grad_normed, normed, scale_vals):
    row_inner = jnp.mean(grad_normed * normed, axis=-1, keepdims=True)
    return scale_vals * (grad_normed - normed * row_inner)


def attend_forward(q_rows, k_rows, v_rows, allowed):
    scores = dot_t(q_rows, k_rows) * HEAD_DIM ** (-0.5)
    scores = jnp.where(allowed, scores, -1e30)
    row_top = jnp.max(scores, axis=-1, keepdims=True)
    exp_vals = jnp.exp(scores - row_top)
    row_total = jnp.sum(exp_vals, axis=-1, keepdims=True)
    prob_vals = (exp_vals / row_total).astype(BF)
    return (dot(prob_vals, v_rows), row_top + jnp.log(row_total))


def attend_backward(q_rows, k_rows, v_rows, g_rows, log_sums, allowed):
    scale = HEAD_DIM ** (-0.5)
    scores = dot_t(q_rows, k_rows) * scale
    scores = jnp.where(allowed, scores, -1e30)
    prob_vals = jnp.exp(scores - log_sums)
    grad_probs = dot_t(g_rows, v_rows)
    row_inner = jnp.sum(prob_vals * grad_probs, axis=-1, keepdims=True)
    grad_scores = (prob_vals * (grad_probs - row_inner)).astype(BF)
    return (
        dot(grad_scores, k_rows) * scale,
        t_dot(grad_scores, q_rows) * scale,
        t_dot(prob_vals.astype(BF), g_rows),
    )


def adam_step(weight, moment_one, moment_two, gradient, step_rate, weight_decay):
    first_new = beta_one * moment_one + (1.0 - beta_one) * gradient
    second_new = beta_two * moment_two + (1.0 - beta_two) * gradient * gradient
    first_hat = first_new / (1.0 - beta_one**STEP)
    second_hat = second_new / (1.0 - beta_two**STEP)
    weight_new = weight - step_rate * (
        first_hat / (jnp.sqrt(second_hat) + adam_eps) + weight_decay * weight
    )
    return (first_new, second_new, weight_new)


def gather_rows(shard):
    return lax.all_gather(shard, OWNERS, axis=0, tiled=False)


def deal(field, axis, dim):
    count = axis_size(axis)
    me = lax.axis_index(axis)
    own = lax.dynamic_index_in_dim(field, me, dim, keepdims=False)
    total = own.astype(F32)
    for step in range(1, count):
        block = lax.dynamic_index_in_dim(field, lax.rem(me + step, count), dim, keepdims=False)
        total = total + send(block.astype(BF), axis, step).astype(F32)
    return total


def scatter_rows(field):
    pre, _, _, _, _, rows, cols = field.shape
    field = deal(field, "c", 4).astype(BF)
    half = cols // 2
    one = deal(field[..., :half], "x", 2).astype(BF)
    one = deal(one.reshape(pre, 4, rows, half), RING_Y, 1)
    two = field[..., half:].transpose(0, 1, 3, 2, 4, 5).reshape(pre, 4, 4, rows, half)
    two = deal(two, RING_Y, 1).astype(BF)
    two = deal(two, "x", 1)
    return jnp.concatenate([one, two], axis=-1)


def on_device(
    layer_input,
    out_cotangent,
    positions,
    qkv_weight,
    qkv_first,
    qkv_second,
    proj_weight,
    proj_first,
    proj_second,
    gate_up_weight,
    gate_up_first,
    gate_up_second,
    down_weight,
    down_first,
    down_second,
    norm_gains,
    gains_first,
    gains_second,
):
    toks = layer_input.shape[1]
    width = layer_input.shape[2]
    length = positions.shape[1]
    q_cols = GROUP * HEAD_DIM
    own_rows = qkv_weight.shape[0]
    hidden = gate_up_weight.shape[1] // (2 * NZ)
    ctx = lax.axis_index(CTX)

    gains_low = norm_gains.astype(BF).astype(F32)
    qkv_low = qkv_weight.astype(BF).astype(F32)
    gate_up_low = gate_up_weight.astype(BF).astype(F32)

    tokens = gather_z(layer_input[0])
    all_pos = jnp.stack(gather_z(positions[0]))

    qkv_scaled = (qkv_low * gains_low[:, :1]).astype(BF)
    q_part, k_part, v_part = jnp.split(
        qkv_scaled, [HEADS * HEAD_DIM, (HEADS + KV_HEADS) * HEAD_DIM], axis=1
    )
    qkv_parts = jnp.concatenate(
        [t.reshape(own_rows, NZ, -1).transpose(1, 0, 2) for t in (q_part, k_part, v_part)], axis=2
    )
    qkv_parts = lax.all_to_all(qkv_parts, "z", split_axis=0, concat_axis=0)
    qkv_use = gather_rows(qkv_parts).transpose(1, 0, 2, 3).reshape(width, -1)
    proj_use = gather_rows(proj_weight.astype(BF)).reshape(q_cols, width)
    gate_up_scaled = (gate_up_low * gains_low[:, 1:]).astype(BF)
    gate_up_parts = (
        gate_up_scaled.reshape(own_rows, 2, NZ, hidden).transpose(2, 0, 1, 3).reshape(NZ, own_rows, -1)
    )
    gate_up_parts = lax.all_to_all(gate_up_parts, "z", split_axis=0, concat_axis=0)
    gate_up_use = gather_rows(gate_up_parts).transpose(1, 0, 2, 3).reshape(width, -1)
    down_use = gather_rows(down_weight.astype(BF)).reshape(hidden, width)
    cotangents = jnp.concatenate(gather_z(out_cotangent[0]))

    own_pos = lax.dynamic_slice_in_dim(all_pos, ctx * toks, toks, axis=1)
    cos_vals, sin_vals = rotary_tables(own_pos.reshape(-1))
    inputs = jnp.concatenate(tokens).astype(F32)
    hidden_one = (inputs * norm_scale(inputs)).astype(BF)
    projected = dot(hidden_one, qkv_use)
    keys = rotate(projected[:, None, q_cols : q_cols + HEAD_DIM], cos_vals, sin_vals)[:, 0]
    key_values = jnp.concatenate([keys, projected[:, q_cols + HEAD_DIM :]], axis=1).astype(BF)
    key_values = lax.all_to_all(
        jnp.broadcast_to(key_values[None], (NCTX, NZ * toks, 2 * HEAD_DIM)),
        CTX,
        split_axis=0,
        concat_axis=0,
    )
    key_values = (
        key_values.reshape(NCTX, NZ, toks, 2 * HEAD_DIM)
        .transpose(1, 0, 2, 3)
        .reshape(NZ, length, 2 * HEAD_DIM)
    )
    queries = rotate(
        projected[:, :q_cols].reshape(NZ * toks, GROUP, HEAD_DIM), cos_vals, sin_vals
    ).astype(BF)
    queries = (
        queries.reshape(NZ, toks, GROUP, HEAD_DIM)
        .transpose(0, 2, 1, 3)
        .reshape(NZ, GROUP * toks, HEAD_DIM)
    )
    keys_all, values_all = key_values[..., :HEAD_DIM], key_values[..., HEAD_DIM:]

    attended, log_sums, masks, branch = [], [], [], []
    for part in (1, 2, 3, 0):
        allowed = all_pos[part][None, :] <= own_pos[part][:, None]
        allowed = jnp.broadcast_to(allowed[None], (GROUP, toks, length)).reshape(-1, length)
        out, log_sum = attend_forward(queries[part], keys_all[part], values_all[part], allowed)
        out = (
            out.reshape(GROUP, toks, HEAD_DIM).transpose(1, 0, 2).reshape(toks, q_cols).astype(BF)
        )
        masks.append(allowed)
        attended.append(out)
        log_sums.append(log_sum)
        branch.append(dot(out, proj_use))
    masks, attended, log_sums, branch = (
        [t[3], t[0], t[1], t[2]] for t in (masks, attended, log_sums, branch)
    )
    middle = layer_input[0].astype(F32) + branch[0]
    for got in return_z([t.astype(BF) for t in branch]):
        middle = middle + got.astype(F32)
    scale_two = norm_scale(middle)
    normed_two = middle * scale_two
    hidden_two = jnp.concatenate(gather_z(normed_two.astype(BF)))

    gate_up = dot(hidden_two, gate_up_use)
    gate_vals, up_vals = gate_up[:, :hidden], gate_up[:, hidden:]
    sig_vals = jax.nn.sigmoid(gate_vals)
    activated = gate_vals * sig_vals
    product = (activated * up_vals).astype(BF)
    grad_product = dot_t(cotangents, down_use)
    grad_gate = grad_product * up_vals * (sig_vals * (1.0 + gate_vals * (1.0 - sig_vals)))
    grad_up = grad_product * activated
    grad_gate_up = jnp.concatenate([grad_gate, grad_up], axis=1).astype(BF)
    grad_hidden = dot_t(grad_gate_up, gate_up_use).reshape(NZ, toks, width)
    grad_mid_norm = grad_hidden[0]
    for got in return_z([t.astype(BF) for t in grad_hidden]):
        grad_mid_norm = grad_mid_norm + got.astype(F32)
    terms = dot(product, down_use).reshape(NZ, toks, width)
    result = middle + terms[0]
    for got in return_z([t.astype(BF) for t in terms]):
        result = result + got.astype(F32)

    grad_down = t_dot(product, cotangents).astype(BF)
    grad_gate_up_w = t_dot(hidden_two, grad_gate_up).astype(BF)
    sum_down = scatter_rows(grad_down.reshape(1, 2, 4, 2, 2, -1, width))[0]
    sum_gate_up = scatter_rows(grad_gate_up_w.reshape(NZ, 2, 4, 2, 2, own_rows, 2 * hidden))
    sum_gate_up = lax.all_to_all(sum_gate_up.astype(BF), "z", split_axis=0, concat_axis=0)
    sum_gate_up = (
        sum_gate_up.astype(F32)
        .reshape(NZ, own_rows, 2, hidden)
        .transpose(1, 2, 0, 3)
        .reshape(own_rows, -1)
    )

    grad_result = out_cotangent[0].astype(F32)
    grad_middle = grad_result + norm_back(grad_mid_norm, normed_two, scale_two)
    grad_branch = gather_z(grad_middle.astype(BF))
    grad_q, grad_kv = [], []
    for part in range(NZ):
        grad_out = dot_t(grad_branch[part], proj_use).astype(BF)
        grad_out = (
            grad_out.reshape(toks, GROUP, HEAD_DIM).transpose(1, 0, 2).reshape(-1, HEAD_DIM)
        )
        one, two, three = attend_backward(
            queries[part],
            keys_all[part],
            values_all[part],
            grad_out,
            log_sums[part],
            masks[part],
        )
        grad_q.append(one.reshape(GROUP, toks, HEAD_DIM).transpose(1, 0, 2))
        grad_kv.append(jnp.concatenate([two, three], axis=1).astype(BF))
    grad_kv = (
        jnp.stack(grad_kv).reshape(NZ, NCTX, toks, 2 * HEAD_DIM).transpose(1, 0, 2, 3)
    )
    grad_kv = lax.all_to_all(grad_kv, CTX, split_axis=0, concat_axis=0)
    grad_kv = jnp.sum(grad_kv.astype(F32), axis=0).reshape(NZ * toks, 2 * HEAD_DIM)
    grad_q = rotate(jnp.concatenate(grad_q), cos_vals, -sin_vals).reshape(NZ * toks, q_cols)
    grad_k = rotate(grad_kv[:, None, :HEAD_DIM], cos_vals, -sin_vals)[:, 0]
    grad_projected = jnp.concatenate([grad_q, grad_k, grad_kv[:, HEAD_DIM:]], axis=1).astype(BF)
    grad_hidden_one = dot_t(grad_projected, qkv_use).reshape(NZ, toks, width)
    grad_in_norm = grad_hidden_one[0]
    for got in return_z([t.astype(BF) for t in grad_hidden_one]):
        grad_in_norm = grad_in_norm + got.astype(F32)
    own_inputs = layer_input[0].astype(F32)
    scale_one = norm_scale(own_inputs)
    input_grad = grad_middle + norm_back(grad_in_norm, own_inputs * scale_one, scale_one)

    grad_proj = t_dot(jnp.concatenate(attended), jnp.concatenate(grad_branch)).astype(BF)
    sum_proj = scatter_rows(grad_proj.reshape(1, 2, 4, 2, 2, own_rows, width))[0]
    grad_qkv = t_dot(hidden_one, grad_projected).astype(BF)
    sum_qkv = scatter_rows(grad_qkv.reshape(NZ, 2, 4, 2, 2, own_rows, -1))
    sum_qkv = lax.all_to_all(sum_qkv.astype(BF), "z", split_axis=0, concat_axis=0).astype(F32)
    sum_qkv = jnp.concatenate(
        [
            t.transpose(1, 0, 2).reshape(own_rows, -1)
            for t in jnp.split(sum_qkv, [q_cols, q_cols + HEAD_DIM], axis=2)
        ],
        axis=1,
    )

    sum_gains = jnp.stack(
        [jnp.sum(qkv_low * sum_qkv, axis=1), jnp.sum(gate_up_low * sum_gate_up, axis=1)], axis=1
    )
    sum_qkv = sum_qkv * gains_low[:, :1]
    sum_gate_up = sum_gate_up * gains_low[:, 1:]
    qkv_new = adam_step(qkv_weight, qkv_first, qkv_second, sum_qkv, rate_qkv, decay_rate)
    proj_new = adam_step(proj_weight, proj_first, proj_second, sum_proj, rate_proj, decay_rate)
    gate_up_new = adam_step(
        gate_up_weight, gate_up_first, gate_up_second, sum_gate_up, rate_gate_up, decay_rate
    )
    down_new = adam_step(down_weight, down_first, down_second, sum_down, rate_down, decay_rate)
    gains_new = adam_step(norm_gains, gains_first, gains_second, sum_gains, rate_gains, 0.0)
    return (
        result.astype(BF)[None],
        input_grad[None],
        *qkv_new,
        *proj_new,
        *gate_up_new,
        *down_new,
        *gains_new,
    )


def solution(mesh):
    inner = Mesh(mesh.devices.reshape(tuple(SIZES.values())), tuple(SIZES))
    rows = P(ROWS, None)
    acts = P(SEQ, CTX, None)
    return jax.shard_map(
        on_device,
        mesh=inner,
        in_specs=(acts, acts, P(SEQ, None)) + (rows,) * 15,
        out_specs=(acts, acts) + (rows,) * 15,
        check_vma=False,
    )
```

time: 4270 us -> 789 us (0.18)
  waiting for transfers between devices: 3060 us -> 254 us
  blocking collectives: 721 us -> 21.3 us
  matrix products: 240 us -> 142 us
  starting transfers between devices: 66.9 us -> 133 us
    reduce_scatter x3 -> x0, waiting for transfers between devices: 2230 us -> none  [the longest x1 988 us: on_device(): lax.psum_scatter(grad_gate_up_term, ('seq', 'ctx'), scatter_dimension=0,...]
    all_gather x6 -> x4, waiting for transfers between devices: 691 us -> 114 us  [gather_rows(): return lax.all_gather(shard, OWNERS, axis=0, tiled=False)]
    unnamed x1 -> x0, blocking collectives: 543 us -> none
    all_gather x1 -> x0, blocking collectives: 178 us -> none  [on_device(): lax.all_gather(norm_gains.astype(jnp.bfloat16), ('seq', 'ctx'), axis=0, t...]
    unnamed x26 -> x4, waiting for transfers between devices: 148 us -> 0.07 us
    ppermute x0 -> x79, starting transfers between devices: none -> 117 us  [send(): lax.ppermute(field, axis, [(i, (i + step) % count) for i in range(count)])]
    ppermute x0 -> x79, waiting for transfers between devices: none -> 116 us  [send(): lax.ppermute(field, axis, [(i, (i + step) % count) for i in range(count)])]
    dot_general x40 -> x42, matrix products: 240 us -> 142 us  [the longest x15 61.4 us: dot_t(): lax.dot_general(lhs, rhs, (((1,), (1,)), ((), ())), preferred_element_typ...]
  transfers between devices with their start and end apart: 23 -> 87, of which waited for: 14 -> 34; matrix products, arithmetic and copies ran while one was open for 18% -> 38% of each run, Pallas kernels for 0% -> 0%
where the time goes in v1:
time: 789 us; the launch traced here: 781 us
  waiting for transfers between devices  254 us (32%)
  matrix products  142 us (18%)
  starting transfers between devices  133 us (17%)
  local copies, waits for them, and re-layouts  119 us (15%)
  other arithmetic  94.2 us (12%)
  blocking collectives  21.3 us (3%)
  between operations  16.6 us (2%)
    ppermute x79, starting transfers between devices, send(): lax.ppermute(field, axis, [(i, (i + step) % count) for i in range(count)])  117 us
    ppermute x79, waiting for transfers between devices, send(): lax.ppermute(field, axis, [(i, (i + step) % count) for i in range(count)])  116 us
    all_gather x4, waiting for transfers between devices, gather_rows(): return lax.all_gather(shard, OWNERS, axis=0, tiled=False)  114 us
    dot_general x15, matrix products, dot_t(): lax.dot_general(lhs, rhs, (((1,), (1,)), ((), ())), preferred_element_typ...  61.4 us
    dot_general x15, matrix products, dot(): return jnp.dot(lhs, rhs, preferred_element_type=F32)  41 us
    dot_general x12, matrix products, t_dot(): lax.dot_general(lhs, rhs, (((0,), (0,)), ((), ())), preferred_element_typ...  39.5 us
    another operation x7, local copies, waits for them, and re-layouts  28.3 us
    unnamed x218, local copies, waits for them, and re-layouts  17.7 us
  transfers between devices with their start and end apart: 87, of which 34 were waited for; matrix products, arithmetic and copies ran while one was open for 38% of the time, Pallas kernels for 0%

profile of v1, /device:TPU:0, one launch (start us, length us, event | category | flops | bytes accessed | tf_op | source)
XLA Modules:
  0.0 780.8 jit_solution(8747854301275846126)
XLA Ops:
  9.4 11.0 %all_to_all.30 = bf16[4,16,640]{2,1,0:T(8,128)(2,1)} all-to-all(bf16[4,16,640]{2,1,0:T(8,128)(2,1)S(1)} %copy.268), channel_id=1, replica_groups=mesh['z'=4,'yh'=2,'x'=4,'yl'=2,'c'=2] {'z'}, dimensions={0} | all-to-all | bytes 163840 | tf_op jit(solution)/shard_map/all_to_all | solution.py:204
  25.9 10.3 %all_to_all.31 = bf16[4,16,2816]{2,1,0:T(8,128)(2,1)} all-to-all(bf16[4,16,2816]{2,1,0:T(8,128)(2,1)S(1)} %reshape.944), channel_id=1, replica_groups=mesh['z'=4,'yh'=2,'x'=4,'yl'=2,'c'=2] {'z'}, dimensions={0} | all-to-all | bytes 720896 | tf_op jit(solution)/shard_map/all_to_all | solution.py:211
  46.5 17.5 %collective-permute-done = s32[2048]{0:T(1024)S(1)} collective-permute-done((s32[2048]{0:T(1024)S(1)}, s32[2048]{0:T(1024)S(1)}, u32[]{:S(2)}, u32[]{:S(2)}) %collective-permute-start) | collective-permute-done | bytes 8224 | tf_op jit(solution)/shard_map/ppermute | solution.py:48
  65.2 12.9 %all-gather.10.cloned.1.call-done = bf16[128,16,640]{2,1,0:T(8,128)(2,1)} async-done(((bf16[4,16,640]{2,1,0:T(8,128)(2,1)}), bf16[128,16,640]{2,1,0:T(8,128)(2,1)}) %all-gather.10.cloned.1.call-update) | async-done | bytes 2621456 | tf_op jit(solution)/shard_map/all_gather | solution.py:136
  102.7 15.9 %all-to-all-done.1 = bf16[16,512,128]{2,1,0:T(8,128)(2,1)S(1)} async-done(((bf16[16,512,128]{2,1,0:T(8,128)(2,1)}), bf16[16,512,128]{2,1,0:T(8,128)(2,1)S(1)}, u32[]{:S(2)}, u32[]{:S(2)}) %all-to-all-start.1) | async-done | bytes 2097184 | tf_op jit(solution)/shard_map/all_to_all | solution.py:223
  134.0 17.8 %all-gather.12.cloned.1.call-done = bf16[512,2048]{1,0:T(8,128)(2,1)} async-done(((bf16[16,2048]{1,0:T(8,128)(2,1)}), bf16[512,2048]{1,0:T(8,128)(2,1)}) %all-gather.12.cloned.1.call-update) | async-done | bytes 2097168 | tf_op jit(solution)/shard_map/all_gather | solution.py:136
  199.2 17.8 %all-gather.16.cloned.1.call-done = bf16[32,44,2048]{2,1,0:T(8,128)(2,1)} async-done(((bf16[1,44,2048]{2,1,0:T(8,128)(2,1)}), bf16[32,44,2048]{2,1,0:T(8,128)(2,1)}) %all-gather.16.cloned.1.call-update) | async-done | bytes 5767184 | tf_op jit(solution)/shard_map/all_gather | solution.py:136
  217.0 8.0 %reshape.1015 = bf16[1408,2048]{1,0:T(8,128)(2,1)} reshape(bf16[32,44,2048]{2,1,0:T(8,128)(2,1)} %all-gather.16.cloned.1.call-done) | data formatting | bytes 11534336
  225.0 65.2 %all-gather.14.cloned.1.call-done = bf16[128,16,2816]{2,1,0:T(8,128)(2,1)} async-done(((bf16[4,16,2816]{2,1,0:T(8,128)(2,1)}), bf16[128,16,2816]{2,1,0:T(8,128)(2,1)}) %all-gather.14.cloned.1.call-update) | async-done | bytes 11534352 | tf_op jit(solution)/shard_map/all_gather | solution.py:136
  297.7 10.2 %fusion.103 = f32[512,2816]{1,0:T(8,128)} fusion(bf16[2048,2816]{1,0:T(8,128)(2,1)S(1)} %bitcast.643, bf16[128,2048]{1,0:T(8,128)(2,1)} %collective-permute-done.11, bf16[128,2048]{1,0:T(8,128)(2,1)} %collective-permute-done.10, bf16[128,2048]{1,0:T(8,128)(2,1)} %collective-permute-done.9, bf16[128,2048]{1,0:T(8,128)(2,1)} %multiply_convert_fusion.7), kind=kOutput, calls=%fused_computation.230 | convolution fusion | flops 5913968640 | bytes 19398656 | tf_op jit(solution)/shard_map/dot_general | solution.py:60
  311.7 10.8 %multiply_convert_fusion.5 = (bf16[512,1408]{1,0:T(8,128)(2,1)}, bf16[512,1408]{1,0:T(8,128)(2,1)}, bf16[512,1408]{1,0:T(8,128)(2,1)S(1)}) fusion(f32[512,2816]{1,0:T(8,128)} %fusion.103, bf16[1408,2048]{1,0:T(8,128)(2,1)} %reshape.1015, bf16[128,2048]{1,0:T(8,128)(2,1)} %collective-permute-done.17, bf16[128,2048]{1,0:T(8,128)(2,1)} %collective-permute-done.16, ...), kind=kOutput, calls=%fused_computation.54 | convolution fusion | flops 2971992064 | bytes 17956864 | tf_op jit(solution)/shard_map/dot_general | solution.py:64
  322.5 9.6 %fusion.226 = (bf16[512,2048]{1,0:T(8,128)(2,1)S(1)}, f32[512,2048]{1,0:T(8,128)}) fusion(bf16[2048,2816]{1,0:T(8,128)(2,1)S(1)} %bitcast.644, bf16[512,1408]{1,0:T(8,128)(2,1)} %get-tuple-element.45, bf16[512,1408]{1,0:T(8,128)(2,1)} %get-tuple-element.44), kind=kOutput, calls=%fused_computation.457 | convolution fusion | flops 5912395776 | bytes 20709376 | tf_op jit(solution)/shard_map/dot_general | solution.py:64
  333.3 7.9 %fusion.227 = (bf16[512,2048]{1,0:T(8,128)(2,1)S(1)}, f32[512,2048]{1,0:T(8,128)}) fusion(bf16[512,1408]{1,0:T(8,128)(2,1)S(1)} %get-tuple-element.50, bf16[1408,2048]{1,0:T(8,128)(2,1)} %reshape.1015), kind=kOutput, calls=%fused_computation.458 | convolution fusion | flops 2953838592 | bytes 13500416 | tf_op jit(solution)/shard_map/dot_general | solution.py:60
  349.2 11.2 %convolution_convert_fusion = bf16[2048,2816]{1,0:T(8,128)(2,1)} fusion(bf16[512,1408]{1,0:T(8,128)(2,1)S(1)} %copy-done.93, bf16[512,1408]{1,0:T(8,128)(2,1)S(1)} %copy-done.92, bf16[128,2048]{1,0:T(8,128)(2,1)} %collective-permute-done.11, bf16[128,2048]{1,0:T(8,128)(2,1)} %collective-permute-done.10, bf16[128,2048]{1,0:T(8,128)(2,1)} %collective-permute-done.9, ...), kind=kOutput, calls=%fused_computation.2 | convolution fusion | flops 5925502976 | bytes 16515072 | tf_op jit(solution)/shard_map/dot_general | solution.py:68
  360.4 9.7 %constant_dynamic-slice_fusion.5 = (bf16[4,2,4,2,1,16,2816]{6,5,4,3,2,1,0:T(8,128)(2,1)}, bf16[4,2,4,2,1,16,2816]{6,5,4,3,2,1,0:T(8,128)(2,1)}) fusion(bf16[4,2,4,2,2,16,2816]{6,5,4,3,2,1,0:T(8,128)(2,1)} %bitcast.645, s32[]{:T(128)S(6)} %select_n.133, s32[]{:T(128)S(6)} %select_n.134), kind=kLoop, calls=%fused_computation.406 | loop fusion | bytes 23068680 | tf_op jit(solution)/shard_map/jit(dynamic_index_in_dim)/dynamic_slice | solution.py:142
  370.1 7.6 convolution_convert_fusion.1
  377.7 8.0 %reshape.980 = bf16[1,2,4,2,2,44,2048]{6,5,4,3,2,1,0:T(8,128)(2,1)} reshape(bf16[1408,2048]{1,0:T(8,128)(2,1)} %convolution_convert_fusion.1) | data formatting | bytes 11534336 | tf_op jit(solution)/shard_map/reshape | solution.py:286
  457.6 6.5 multiply_reduce_fusion
  512.4 6.5 copy.320
  540.4 13.3 %collective-permute-done.47 = bf16[1,4,16,1024]{3,2,1,0:T(8,128)(2,1)S(1)} collective-permute-done((bf16[1,4,16,1024]{3,2,1,0:T(8,128)(2,1)S(1)}, bf16[1,4,16,1024]{3,2,1,0:T(8,128)(2,1)S(1)}, u32[]{:S(2)}, u32[]{:S(2)}) %collective-permute-start.47) | collective-permute-done | bytes 131104 | tf_op jit(solution)/shard_map/ppermute | solution.py:48
  553.7 7.5 collective-permute-start.41
  641.1 7.2 collective-permute-done.24
  649.3 9.3 %collective-permute-done.25 = bf16[128,2048]{1,0:T(8,128)(2,1)S(1)} collective-permute-done((bf16[128,2048]{1,0:T(8,128)(2,1)S(1)}, bf16[128,2048]{1,0:T(8,128)(2,1)S(1)}, u32[]{:S(2)}, u32[]{:S(2)}) %collective-permute-start.25) | collective-permute-done | bytes 524320 | tf_op jit(solution)/shard_map/ppermute | solution.py:48
  712.9 20.8 %collective-permute-done.60 = bf16[4,4,16,1408]{3,2,1,0:T(8,128)(2,1)} collective-permute-done((bf16[4,4,16,1408]{3,2,1,0:T(8,128)(2,1)}, bf16[4,4,16,1408]{3,2,1,0:T(8,128)(2,1)}, u32[]{:S(2)}, u32[]{:S(2)}) %collective-permute-start.60) | collective-permute-done | bytes 720928 | tf_op jit(solution)/shard_map/ppermute | solution.py:48
  (603 shorter events, 441.8 us)
Async XLA Ops:
  7.2 70.8 %all-gather.10.cloned.1.call-start = ((), (), s32[]{:S(2)}) async-start(), calls=%async_computation.6 | async-start | bytes 2703360 | tf_op jit(solution)/shard_map/all_gather | solution.py:136
  20.4 131.3 %all-gather.12.cloned.1.call-start = ((), (), s32[]{:S(2)}) async-start(), calls=%async_computation.7 | async-start | bytes 2162688 | tf_op jit(solution)/shard_map/all_gather | solution.py:136
  22.0 195.0 %all-gather.16.cloned.1.call-start = ((), (), s32[]{:S(2)}) async-start(), calls=%async_computation.9 | async-start | bytes 6488064 | tf_op jit(solution)/shard_map/all_gather | solution.py:136
  23.8 266.4 %all-gather.14.cloned.1.call-start = ((), (), s32[]{:S(2)}) async-start(), calls=%async_computation.8 | async-start | bytes 11894784 | tf_op jit(solution)/shard_map/all_gather | solution.py:136
  45.2 262.7 %collective-permute-start.17 = (bf16[128,2048]{1,0:T(8,128)(2,1)}, bf16[128,2048]{1,0:T(8,128)(2,1)}, u32[]{:S(2)}, u32[]{:S(2)}) collective-permute-start(bf16[128,2048]{1,0:T(8,128)(2,1)} %bitcast.58), channel_id=1, source_target_pairs={{0,96},{32,0},{64,32},{96,64},{1,97},{33,1},{65,33},{97,65},{2,98}... | collective-permute-start | bytes 1572872 | tf_op jit(solution)/shard_map/ppermute | solution.py:48
  63.9 244.0 %collective-permute-start.16 = (bf16[128,2048]{1,0:T(8,128)(2,1)}, bf16[128,2048]{1,0:T(8,128)(2,1)}, u32[]{:S(2)}, u32[]{:S(2)}) collective-permute-start(bf16[128,2048]{1,0:T(8,128)(2,1)} %bitcast.58), channel_id=1, source_target_pairs={{0,64},{32,96},{64,0},{96,32},{1,65},{33,97},{65,1},{97,33},{2,66}... | collective-permute-start | bytes 1572872 | tf_op jit(solution)/shard_map/ppermute | solution.py:48
  85.4 33.1 %all-to-all-start.1 = ((bf16[16,512,128]{2,1,0:T(8,128)(2,1)}), bf16[16,512,128]{2,1,0:T(8,128)(2,1)S(1)}, u32[]{:S(2)}, u32[]{:S(2)}) async-start(bf16[16,512,128]{2,1,0:T(8,128)(2,1)} %broadcast_in_dim.31), calls=%async_computation.1 | async-start | bytes 4194304 | tf_op jit(solution)/shard_map/all_to_all | solution.py:223
  153.8 35.5 %collective-permute-start.8 = (bf16[128,2048]{1,0:T(8,128)(2,1)S(1)}, bf16[128,2048]{1,0:T(8,128)(2,1)S(1)}, u32[]{:S(2)}, u32[]{:S(2)}) collective-permute-start(bf16[128,2048]{1,0:T(8,128)(2,1)S(1)} %convolution_convert_fusion.4), channel_id=1, source_target_pairs={{0,32},{32,64},{64,96},{96,0},{1,33},{33,65},{65,97},{97,1},{2,34}... | collective-permute-start | bytes 1572872 | tf_op jit(solution)/shard_map/ppermute | solution.py:48
  194.7 101.4 %collective-permute-start.11 = (bf16[128,2048]{1,0:T(8,128)(2,1)}, bf16[128,2048]{1,0:T(8,128)(2,1)}, u32[]{:S(2)}, u32[]{:S(2)}) collective-permute-start(bf16[128,2048]{1,0:T(8,128)(2,1)} %multiply_convert_fusion.7), channel_id=1, source_target_pairs={{0,96},{32,0},{64,32},{96,64},{1,97},{33,1},{65,33},{97,65},{2,98}... | collective-permute-start | bytes 1572872 | tf_op jit(solution)/shard_map/ppermute | solution.py:48
  197.6 100.1 %collective-permute-start.10 = (bf16[128,2048]{1,0:T(8,128)(2,1)}, bf16[128,2048]{1,0:T(8,128)(2,1)}, u32[]{:S(2)}, u32[]{:S(2)}) collective-permute-start(bf16[128,2048]{1,0:T(8,128)(2,1)} %multiply_convert_fusion.7), channel_id=1, source_target_pairs={{0,64},{32,96},{64,0},{96,32},{1,65},{33,97},{65,1},{97,33},{2,66}... | collective-permute-start | bytes 1572872 | tf_op jit(solution)/shard_map/ppermute | solution.py:48
  198.6 99.1 %collective-permute-start.9 = (bf16[128,2048]{1,0:T(8,128)(2,1)}, bf16[128,2048]{1,0:T(8,128)(2,1)}, u32[]{:S(2)}, u32[]{:S(2)}) collective-permute-start(bf16[128,2048]{1,0:T(8,128)(2,1)} %multiply_convert_fusion.7), channel_id=1, source_target_pairs={{0,32},{32,64},{64,96},{96,0},{1,33},{33,65},{65,97},{97,1},{2,34}... | collective-permute-start | bytes 1572872 | tf_op jit(solution)/shard_map/ppermute | solution.py:48
  342.4 59.7 %collective-permute-start.12 = (bf16[128,2048]{1,0:T(8,128)(2,1)}, bf16[128,2048]{1,0:T(8,128)(2,1)}, u32[]{:S(2)}, u32[]{:S(2)}) collective-permute-start(bf16[128,2048]{1,0:T(8,128)(2,1)} %get-tuple-element.67), channel_id=1, source_target_pairs={{0,96},{32,0},{64,32},{96,64},{1,97},{33,1},{65,33},{97,65},{2,98}... | collective-permute-start | bytes 1572872 | tf_op jit(solution)/shard_map/ppermute | solution.py:48
  344.1 57.9 %collective-permute-start.14 = (bf16[128,2048]{1,0:T(8,128)(2,1)}, bf16[128,2048]{1,0:T(8,128)(2,1)}, u32[]{:S(2)}, u32[]{:S(2)}) collective-permute-start(bf16[128,2048]{1,0:T(8,128)(2,1)} %get-tuple-element.68), channel_id=1, source_target_pairs={{0,32},{32,64},{64,96},{96,0},{1,33},{33,65},{65,97},{97,1},{2,34}... | collective-permute-start | bytes 1572872 | tf_op jit(solution)/shard_map/ppermute | solution.py:48
  344.4 41.3 %collective-permute-start.18 = (bf16[128,2048]{1,0:T(8,128)(2,1)}, bf16[128,2048]{1,0:T(8,128)(2,1)}, u32[]{:S(2)}, u32[]{:S(2)}) collective-permute-start(bf16[128,2048]{1,0:T(8,128)(2,1)} %get-tuple-element.64), channel_id=1, source_target_pairs={{0,96},{32,0},{64,32},{96,64},{1,97},{33,1},{65,33},{97,65},{2,98}... | collective-permute-start | bytes 1572872 | tf_op jit(solution)/shard_map/ppermute | solution.py:48
  347.4 52.4 %collective-permute-start.20 = (bf16[128,2048]{1,0:T(8,128)(2,1)}, bf16[128,2048]{1,0:T(8,128)(2,1)}, u32[]{:S(2)}, u32[]{:S(2)}) collective-permute-start(bf16[128,2048]{1,0:T(8,128)(2,1)} %get-tuple-element.65), channel_id=1, source_target_pairs={{0,32},{32,64},{64,96},{96,0},{1,33},{33,65},{65,97},{97,1},{2,34}... | collective-permute-start | bytes 1572872 | tf_op jit(solution)/shard_map/ppermute | solution.py:48
  347.8 52.0 %collective-permute-start.19 = (bf16[128,2048]{1,0:T(8,128)(2,1)}, bf16[128,2048]{1,0:T(8,128)(2,1)}, u32[]{:S(2)}, u32[]{:S(2)}) collective-permute-start(bf16[128,2048]{1,0:T(8,128)(2,1)} %get-tuple-element.66), channel_id=1, source_target_pairs={{0,64},{32,96},{64,0},{96,32},{1,65},{33,97},{65,1},{97,33},{2,66}... | collective-permute-start | bytes 1572872 | tf_op jit(solution)/shard_map/ppermute | solution.py:48
  399.7 184.7 %collective-permute-start.66 = (bf16[1,2,4,2,44,2048]{5,2,4,3,1,0:T(4,128)(2,1)}, bf16[1,2,4,2,44,2048]{5,2,4,3,1,0:T(4,128)(2,1)}, u32[]{:S(2)}, u32[]{:S(2)}) collective-permute-start(bf16[1,2,4,2,44,2048]{5,2,4,3,1,0:T(4,128)(2,1)} %copy.314), channel_id=1, source_target_pairs={{0,1},{1,0},{2,3},{3,2},{4,5},{5,4},{6,7},{7,6},{8,9},{9,8},{10,11... | collective-permute-start | bytes 8650760 | tf_op jit(solution)/shard_map/ppermute | solution.py:48
  399.7 296.1 %collective-permute-start.53 = (bf16[4,2,4,2,16,2816]{5,4,2,3,1,0:T(8,128)(2,1)}, bf16[4,2,4,2,16,2816]{5,4,2,3,1,0:T(8,128)(2,1)}, u32[]{:S(2)}, u32[]{:S(2)}) collective-permute-start(bf16[4,2,4,2,16,2816]{5,4,2,3,1,0:T(8,128)(2,1)} %bitcast.607), channel_id=1, source_target_pairs={{0,1},{1,0},{2,3},{3,2},{4,5},{5,4},{6,7},{7,6},{8,9},{9,8},{10,11... | collective-permute-start | bytes 17301512 | tf_op jit(solution)/shard_map/ppermute | solution.py:48
  406.1 49.4 %collective-permute-start.23 = (bf16[128,2048]{1,0:T(8,128)(2,1)}, bf16[128,2048]{1,0:T(8,128)(2,1)}, u32[]{:S(2)}, u32[]{:S(2)}) collective-permute-start(bf16[128,2048]{1,0:T(8,128)(2,1)} %get-tuple-element.32), channel_id=1, source_target_pairs={{0,96},{32,0},{64,32},{96,64},{1,97},{33,1},{65,33},{97,65},{2,98}... | collective-permute-start | bytes 1572872 | tf_op jit(solution)/shard_map/ppermute | solution.py:48
  409.3 64.2 %collective-permute-start.22 = (bf16[128,2048]{1,0:T(8,128)(2,1)}, bf16[128,2048]{1,0:T(8,128)(2,1)}, u32[]{:S(2)}, u32[]{:S(2)}) collective-permute-start(bf16[128,2048]{1,0:T(8,128)(2,1)} %get-tuple-element.32), channel_id=1, source_target_pairs={{0,64},{32,96},{64,0},{96,32},{1,65},{33,97},{65,1},{97,33},{2,66}... | collective-permute-start | bytes 1572872 | tf_op jit(solution)/shard_map/ppermute | solution.py:48
  496.6 36.7 %collective-permute-start.40 = (bf16[1,2,4,2,16,2048]{5,4,3,2,1,0:T(8,128)(2,1)}, bf16[1,2,4,2,16,2048]{5,4,3,2,1,0:T(8,128)(2,1)}, u32[]{:S(2)}, u32[]{:S(2)}) collective-permute-start(bf16[1,2,4,2,16,2048]{5,4,3,2,1,0:T(8,128)(2,1)} %dynamic-slice_bitcast_fusion.1), channel_id=1, source_target_pairs={{0,1},{1,0},{2,3},{3,2},{4,5},{5,4},{6,7},{7,6},{8,9},{9,8},{10,11... | collective-permute-start | bytes 3145736 | tf_op jit(solution)/shard_map/ppermute | solution.py:48
  528.4 67.7 %all-to-all-start.3 = ((bf16[16,4,128,128]{2,3,1,0:T(8,128)(2,1)}), bf16[16,4,128,128]{2,3,1,0:T(8,128)(2,1)}, u32[]{:S(2)}, u32[]{:S(2)}) async-start(bf16[16,4,128,128]{2,3,1,0:T(8,128)(2,1)} %copy.299), calls=%async_computation.3 | async-start | bytes 4194304 | tf_op jit(solution)/shard_map/all_to_all | solution.py:318
  609.9 49.2 %collective-permute-start.27 = (bf16[4,2,4,2,16,640]{5,4,2,3,1,0:T(8,128)(2,1)S(1)}, bf16[4,2,4,2,16,640]{5,4,2,3,1,0:T(8,128)(2,1)S(1)}, u32[]{:S(2)}, u32[]{:S(2)}) collective-permute-start(bf16[4,2,4,2,16,640]{5,4,2,3,1,0:T(8,128)(2,1)S(1)} %bitcast.669), channel_id=1, source_target_pairs={{0,1},{1,0},{2,3},{3,2},{4,5},{5,4},{6,7},{7,6},{8,9},{9,8},{10,11... | collective-permute-start | bytes 3932168 | tf_op jit(solution)/shard_map/ppermute | solution.py:48
  709.6 29.7 %collective-permute-start.54 = (bf16[4,2,2,16,1408]{4,3,2,1,0:T(8,128)(2,1)S(1)}, bf16[4,2,2,16,1408]{4,3,2,1,0:T(8,128)(2,1)S(1)}, u32[]{:S(2)}, u32[]{:S(2)}) collective-permute-start(bf16[4,2,2,16,1408]{4,3,2,1,0:T(8,128)(2,1)S(1)} %get-tuple-element.53), channel_id=1, source_target_pairs={{0,4},{4,8},{8,12},{12,0},{1,5},{5,9},{9,13},{13,1},{2,6},{6,10},{... | collective-permute-start | bytes 2162696 | tf_op jit(solution)/shard_map/ppermute | solution.py:48
  (167 other events, 2206.3 us)
Sparse Core Ops, SparseCore 0:
  20.5 57.4 all-gather.9
  80.3 71.3 all-gather.11
  154.0 62.9 all-gather.15
  218.5 71.5 all-gather.13
